TPU v7x, 512 devices: a whole 4x4x16 slice. The times are simulated.
512 devices in a mesh: lon: 16 (over y, x), lat: 32 (over z, core).
Axes of the slice: x: 4, y: 4, z: 16, core: 2. Of those that a mesh axis runs over, the one named last changes fastest.
Arguments:
- vorticity: float32 [8, 2, 768, 3072], P(None, None, 'lat', 'lon'), may hold values from -6 to 6
- legendre_table: float32 [768, 512, 1025], P('lat', 'lon'), may hold values from -0.15625 to 0.15625
- pair_slots: int32 [512], replicated, may hold values from 0 to 511, each once
- diffusion: float32 [8], replicated, may hold values from 0.3 to 3
Outputs:
- spectrum: float32 [512, 8, 2, 1025], P('lon')
Inputs may be any that keep to these rules, and one draw needn't show every extreme that they name: Each pair appears in exactly one slot; slot s holds the wavenumbers pair_slots[s] and 1023 - pair_slots[s].
All inputs are finite; a program needn't handle non-finite values.
Results may differ from a plain program's by a relative error of at most 0.0003.
Values sent between devices are 32-bit elements; how exact they have to be, the bound alone decides.
A program may use at most 64 MiB of HBM per device.

v0:
```python
import math

import jax
import jax.numpy as jnp
from jax import lax
from jax.sharding import PartitionSpec as P

two_pi = 2.0 * math.pi


def legendre(fourier_six, wave_table, pair_ids, wave_count):
    northern = fourier_six[:, :, :, :, 0, :]
    southern = fourier_six[:, :, :, :, 1, :]
    stacked = jnp.stack([northern + southern, northern - southern], axis=1)
    projected = jnp.einsum(
        "spwrlj,jsc->spwlrc", stacked, wave_table, precision=lax.Precision.HIGHEST
    )
    columns = jnp.arange(wave_table.shape[2], dtype=jnp.int32)
    first_len = wave_count - pair_ids[:, None]
    second = columns[None, :] >= first_len
    offset = jnp.where(second, columns[None, :] - first_len, columns[None, :])
    odd_mask = offset % 2 == 1
    chosen = jnp.where(second[:, None, None, None, :], projected[:, :, 1], projected[:, :, 0])
    return jnp.where(odd_mask[:, None, None, :], chosen[:, 1], chosen[:, 0])


def apply_damping(values, pair_ids, diffusion, wave_count):
    columns = jnp.arange(values.shape[3], dtype=jnp.int32)
    second = columns[None, :] >= wave_count - pair_ids[:, None]
    degree = jnp.where(second, columns[None, :] - 1, pair_ids[:, None] + columns[None, :]).astype(
        jnp.float32
    )
    degree_ratio = degree * (degree + 1.0) / float((wave_count - 1) * wave_count)
    damping = 1.0 / (1.0 + diffusion[None, :, None, None] * (degree_ratio**2)[:, None, None, :])
    return values * damping


def per_device(vorticity, legendre_table, pair_slots, diffusion):
    levels, hemispheres, band_rows, local_lon = vorticity.shape
    lon_count = lax.axis_size("lon")
    full_lon = local_lon * lon_count
    grid_rows = vorticity.reshape(levels * hemispheres * band_rows, local_lon)
    slot_here = legendre_table.shape[1]
    wave_count = pair_slots.shape[0] * 2
    norm_scale = 1.0 / math.sqrt(full_lon)
    lon_start = lax.axis_index("lon") * local_lon
    wave_ids = jnp.stack([pair_slots, wave_count - 1 - pair_slots], axis=1)
    positions = lon_start + jnp.arange(local_lon, dtype=jnp.int32)
    phase_ids = wave_ids[:, :, None] * positions[None, None, :] % full_lon
    angles = phase_ids.astype(jnp.float32) * (two_pi / full_lon)
    wave_table = jnp.stack([jnp.cos(angles), -jnp.sin(angles)], axis=2).reshape(
        4 * slot_here * lax.axis_size("lon"), local_lon
    )
    product = lax.dot_general(
        wave_table,
        grid_rows,
        (((1,), (1,)), ((), ())),
        precision=lax.Precision.HIGHEST,
        preferred_element_type=jnp.float32,
    )
    fourier = lax.psum_scatter(product * norm_scale, "lon", scatter_dimension=0, tiled=True)
    fourier_six = fourier.reshape(slot_here, 2, 2, levels, hemispheres, band_rows)
    lon_pairs = lax.dynamic_slice_in_dim(pair_slots, lax.axis_index("lon") * slot_here, slot_here)
    band_partial = legendre(fourier_six, legendre_table, lon_pairs, wave_count)
    summed = lax.psum(band_partial, "lat")
    return apply_damping(summed, lon_pairs, diffusion, wave_count)


def solution(mesh):
    placed = (P(None, None, "lat", "lon"), P("lat", "lon", None), P(), P())
    return jax.shard_map(
        per_device,
        mesh=mesh,
        in_specs=placed,
        out_specs=P("lon", None, None, None),
        check_vma=False,
    )
```

profile of v0, /device:TPU:1, one launch (start us, length us, event | category | flops | bytes accessed | tf_op | source)
XLA Modules:
  0.0 367.9 jit_solution(6283256095669304718)
XLA Ops:
  6.5 0.0 copy-start
  6.5 0.0 reduce-scatter.2.cloned.1.call-start
  6.5 0.8 broadcast_subtract_fusion
  7.4 0.9 pad_add_fusion
  8.2 3.2 fusion.10
  11.5 1.3 pad_maximum_fusion
  12.8 4.0 %copy.20 = f32[512,2,2,192]{3,2,1,0:T(2,128)} copy(f32[512,2,2,192]{0,3,2,1:T(8,128)} %pad_maximum_fusion) | data formatting | bytes 3145728 | tf_op jit(solution)/shard_map/stack | solution.py:51
  16.8 3.6 reshape.215
  20.4 6.7 %convolution_multiply_fusion = f32[2048,384]{1,0:T(8,128)} fusion(f32[2048,192]{1,0:T(8,128)} %reshape.215, f32[384,192]{1,0:T(8,128)} %bitcast.39), kind=kOutput, calls=%fused_computation.5 | convolution fusion | flops 1812725760 | bytes 5013504 | tf_op jit(solution)/shard_map/dot_general | solution.py:54
  27.1 0.0 reduce-scatter.2.cloned.1.call-update
  27.2 0.2 all-reduce.2.cloned.1.call-start
  27.4 0.8 broadcast_subtract_fusion.1
  28.2 0.8 fusion.13
  29.0 93.1 %reduce-scatter.2.cloned.1.call-done = f32[128,384]{1,0:T(8,128)} async-done(((f32[2048,384]{1,0:T(8,128)}), f32[128,384]{1,0:T(8,128)}) %reduce-scatter.2.cloned.1.call-update) | async-done | bytes 196624 | tf_op jit(solution)/shard_map/reduce_scatter | solution.py:61
  122.0 3.6 reshape.217
  125.7 2.7 fusion.17
  128.3 0.1 add_bitcast_fusion
  128.4 0.0 copy-done
  128.4 0.0 copy-start.2
  128.4 9.0 %convolution_bitcast_fusion = f32[32,2,2,8,2,1025]{5,3,4,2,1,0:T(8,128)S(1)} fusion(f32[24,32,1025,1,1,1]{2,1,0,5,4,3:T(8,128)S(1)} %bitcast.36, f32[32,1,2,2,8,24]{5,4,3,2,1,0:T(8,128)S(1)} %get-tuple-element.8, f32[32,1,2,2,8,24]{5,4,3,2,1,0:T(8,128)S(1)} %get-tuple-element.7), kind=kOutput, calls=%fused_computation | convolution fusion | flops 604618752 | bytes 11742208 | tf_op jit(solution)/shard_map/spwrlj,jsc->spwlrc/dot_general | solution.py:15
  137.4 0.0 copy-done.2
  137.4 0.0 copy-start.1
  137.4 0.8 fusion
  138.3 0.0 copy-done.1
  138.3 1.7 fusion.2
  140.0 0.0 all-reduce.2.cloned.1.call-update
  140.0 0.1 fusion.15
  140.1 0.5 copy-done.3
  140.6 1.3 add_divide_fusion
  141.9 214.4 %all-reduce.2.cloned.1.call-done = f32[32,8,2,1025]{3,1,2,0:T(8,128)} async-done(((f32[32,8,2,1025]{3,1,2,0:T(8,128)}), f32[32,8,2,1025]{3,1,2,0:T(8,128)}) %all-reduce.2.cloned.1.call-update) | async-done | bytes 2099216 | tf_op jit(solution)/shard_map/psum | solution.py:65
  356.3 2.2 broadcast_multiply_fusion
  358.5 2.6 copy.27
  (3 shorter events, 0.0 us)
Async XLA Ops:
  6.5 121.9 %copy-start = (f32[24,32,1025]{2,1,0:T(8,128)S(1)}, f32[24,32,1025]{2,1,0:T(8,128)}, u32[]{:S(2)}) copy-start(f32[24,32,1025]{2,1,0:T(8,128)} %param.5) | copy-start | bytes 9446404
  6.5 115.5 %reduce-scatter.2.cloned.1.call-start = ((), (), s32[]{:S(2)}) async-start(), calls=%async_computation.1 | async-start | bytes 3342336 | tf_op jit(solution)/shard_map/reduce_scatter | solution.py:61
  27.2 329.1 %all-reduce.2.cloned.1.call-start = ((), (), s32[]{:S(2)}) async-start(), calls=%async_computation.2 | async-start | bytes 4718592 | tf_op jit(solution)/shard_map/psum | solution.py:65
  128.4 9.0 %copy-start.2 = (pred[32,1025]{1,0:T(8,128)(4,1)S(1)}, pred[32,1025]{1,0:T(8,128)(4,1)}, u32[]{:S(2)}) copy-start(pred[32,1025]{1,0:T(8,128)(4,1)} %get-tuple-element.14) | copy-start | bytes 98404
  137.4 0.8 copy-start.1
  140.0 0.7 copy-start.3
Sparse Core Ops, SparseCore 0:
  27.3 94.7 reduce-scatter.1
  140.1 216.1 all-reduce.1
where the time goes:
time: 368 us
  waiting for transfers between devices  308 us (84%)
  local copies, waits for them, and re-layouts  17 us (5%)
  matrix products  15.7 us (4%)
  other arithmetic  13.9 us (4%)
  between operations  13.5 us (4%)
    psum x1, waiting for transfers between devices, per_device(): summed = lax.psum(band_partial, 'lat')  214 us
    reduce_scatter x1, waiting for transfers between devices, per_device(): lax.psum_scatter(product * norm_scale, 'lon', scatter_dimension=0, tiled=...  93.1 us
    dot_general x1, matrix products, legendre(): jnp.einsum('spwrlj,jsc->spwlrc', stacked, wave_table, precision=lax.Preci...  8.98 us
  transfers between devices with their start and end apart: 2, of which 2 were waited for; matrix products, arithmetic and copies ran while one was open for 1% of the time, Pallas kernels for 0%

commit v1 on v0

v1 whole, which is shorter than its diff:
```python
import functools
import math

import jax
import jax.numpy as jnp
import numpy as np
from jax import lax
from jax.experimental import pallas as pl
from jax.experimental.pallas import tpu as pltpu
from jax.sharding import PartitionSpec as P

MESH = pl.DeviceIdType.MESH
F32 = jnp.float32
BF16 = jnp.bfloat16


def real_dft(parts):
    n = len(parts)
    if n == 1:
        return [(parts[0], None)]
    even, odd = real_dft(parts[0::2]), real_dft(parts[1::2])
    out = [None] * (n // 2 + 1)
    for k in range(n // 4 + 1):
        er, ei = even[k]
        orr, oi = odd[k]
        if k == 0:
            out[0] = (er + orr, None)
            out[n // 2] = (er - orr, None)
        elif 4 * k == n:
            out[k] = (er, -orr)
        else:
            c, s = math.cos(2 * math.pi * k / n), math.sin(2 * math.pi * k / n)
            tr, ti = c * orr, -s * orr
            if oi is not None:
                tr, ti = tr + s * oi, ti + c * oi
            ei = 0.0 if ei is None else ei
            out[k] = (er + tr, ei + ti)
            out[n // 2 - k] = (er - tr, ti - ei)
    return out


def class_blocks(k, blocks):
    rows = [(0, k, 0, 0), (0, k, 1, 0), (1, blocks - 1 - k, 0, 0), (1, blocks - 1 - k, 1, 0)]
    if 0 < k < blocks // 2:
        rows += [(0, blocks - k, 0, 1), (0, blocks - k, 1, 1), (1, k - 1, 0, 1), (1, k - 1, 1, 1)]
    return rows


def twiddles(blocks, width, waves):
    full = blocks * width
    per_class = waves // 2 // blocks
    half = blocks // 2
    table = np.zeros((2 * half, 8 * per_class, width))
    position = np.arange(width)
    for k in range(half + 1):
        for at, (second, residue, part, conj) in enumerate(class_blocks(k, blocks)):
            pair = np.arange(per_class) * blocks + residue
            wave = waves - 1 - pair if second else pair
            angle = 2 * np.pi * ((wave[:, None] * position[None, :]) % full) / full
            cos, sin = np.cos(angle) / math.sqrt(full), np.sin(angle) / math.sqrt(full)
            sign = -1.0 if conj else 1.0
            rows = slice(at * per_class, (at + 1) * per_class)
            table[k, rows] = -sin if part else cos
            if 0 < k < half:
                table[half + k, rows] = sign * (cos if part else sin)
    return table.astype(np.float32)


def split(values):
    high = values.astype(BF16)
    return high, (values - high.astype(F32)).astype(BF16)


def dot_t(a, b):
    return lax.dot_general(a, b, (((1,), (1,)), ((), ())), preferred_element_type=F32)


def kernel(
    dims, pair_ref, diff_ref, vort_hbm, table_hbm, twid_hbm, out_hbm,
    vort, table, tail, twid, twid_split, cat, s1, r1, g, s2, r2, part, sib, ring, final,
    load_sem, tab_sem, out_sem, s1_send, s1_recv, s2_send, s2_recv, sib_send, sib_recv,
    rs_send, rs_recv, ag_send, ag_recv, as_send, as_recv,
):
    blocks, depth, levels, band, width, slots, waves, cw = dims
    half, hops = blocks // 2, depth // 2
    tiles = waves // cw
    pad = 32
    per_class = waves // 2 // blocks
    main_rows = 2 * tiles * levels
    pieces = ((0, main_rows // 2, hops), (main_rows // 2, main_rows // 2 + levels, hops - 1))

    me = lax.axis_index("lon")
    lat = lax.axis_index("lat")
    z, core = lat // 2, lat % 2
    other = 1 - core

    def at_z(step):
        return lax.rem(z + step + depth, depth)

    def z_device(step):
        return (me, at_z(step) * 2 + core)

    sibling = (me, z * 2 + other)

    load = pltpu.make_async_copy(vort_hbm, vort, load_sem.at[0])
    load.start()
    load_twid = pltpu.make_async_copy(twid_hbm, twid, load_sem.at[1])
    load_twid.start()

    def table_copy(k):
        if k == tiles:
            return pltpu.make_async_copy(table_hbm.at[:, pl.ds(waves, 1)], tail, tab_sem.at[k])
        return pltpu.make_async_copy(
            table_hbm.at[:, pl.ds(k * cw, cw)], table.at[k, pl.ds(0, band * slots)], tab_sem.at[k]
        )

    for k in range(tiles + 1):
        table_copy(k).start()

    barrier = pltpu.get_barrier_semaphore()

    def greet(k, carry):
        peer = lax.rem(me + k, blocks)
        pl.semaphore_signal(barrier, inc=1, device_id=(peer, lat), device_id_type=MESH)
        return carry

    lax.fori_loop(1, blocks, greet, 0)
    for target in (z_device(1), z_device(-1), sibling):
        pl.semaphore_signal(barrier, inc=1, device_id=target, device_id_type=MESH)

    load.wait()
    for level in range(levels):
        north = vort[pl.ds(2 * level * band, band), :]
        south = vort[pl.ds((2 * level + 1) * band, band), :]
        s1[level] = north + south
        s1[levels + level] = north - south

    pl.semaphore_wait(barrier, blocks + 2)

    def send1(k):
        peer = lax.rem(me + k, blocks)
        return pltpu.make_async_remote_copy(
            src_ref=s1.at[peer], dst_ref=r1.at[me], send_sem=s1_send.at[peer],
            recv_sem=s1_recv.at[me], device_id=(peer, lat), device_id_type=MESH,
        )

    def recv1(k):
        peer = lax.rem(me + k, blocks)
        return pltpu.make_async_remote_copy(
            src_ref=s1.at[peer], dst_ref=r1.at[peer], send_sem=s1_send.at[peer],
            recv_sem=s1_recv.at[peer], device_id=(peer, lat), device_id_type=MESH,
        )

    def loop(low, high, body):
        def step(k, carry):
            body(k)
            return carry

        lax.fori_loop(low, high, step, 0)

    loop(1, blocks, lambda k: send1(k).start())
    r1[me] = s1[me]

    for k in range(tiles + 1):
        table_copy(k).wait()
    table[tiles, pl.ds(0, band * slots), :] = jnp.broadcast_to(tail[...], (band * slots, cw))

    def stack_table(s):
        for k in range(tiles + 1):
            rows = table[k, pl.ds(s, band, stride=slots), :]
            if band < pad:
                rows = jnp.concatenate([rows, jnp.zeros((pad - band, cw), F32)], axis=0)
            high, low = split(rows)
            lanes = pl.ds(k * cw, cw)
            cat[s, pl.ds(0, pad), lanes] = high
            cat[s, pl.ds(pad, pad), lanes] = high
            cat[s, pl.ds(2 * pad, pad), lanes] = low

    loop(0, slots, stack_table)

    load_twid.wait()

    def split_twiddles(k):
        high, low = split(twid[k])
        twid_split[0, k] = high
        twid_split[1, k] = low

    loop(0, 2 * half, split_twiddles)
    loop(1, blocks, lambda k: recv1(k).wait_recv())

    spectrum = real_dft([r1[a] for a in range(blocks)])
    for k in range(half + 1):
        rows = class_blocks(k, blocks)
        count = len(rows) * per_class
        total = None
        for number, value in ((k, spectrum[k][0]), (half + k, spectrum[k][1])):
            if value is None:
                continue
            if band < pad:
                value = jnp.concatenate([value, jnp.zeros((pad - band, width), F32)], axis=0)
            high, low = split(value)
            w_high = twid_split[0, number, pl.ds(0, count), :]
            w_low = twid_split[1, number, pl.ds(0, count), :]
            term = dot_t(w_high, high) + (dot_t(w_high, low) + dot_t(w_low, high))
            total = term if total is None else total + term
        for at, (second, residue, which, _) in enumerate(rows):
            g[pl.ds(residue * per_class, per_class), pl.ds((2 * second + which) * pad, pad)] = total[
                at * per_class : (at + 1) * per_class
            ]

    unroll = 8

    def gather(i):
        for j in range(unroll):
            pair = pair_ref[i * unroll + j]
            row = (pair & (blocks - 1)) * per_class + (pair >> (blocks.bit_length() - 1))
            s2[pl.ds(i * unroll + j, 1), :] = g[pl.ds(row, 1), :]

    loop(0, waves // 2 // unroll, gather)

    def block_of(index):
        return pl.ds(pl.multiple_of(index * slots, 8), slots)

    def copy2(k, incoming):
        peer = lax.rem(me + k, blocks)
        return pltpu.make_async_remote_copy(
            src_ref=s2.at[block_of(peer)], dst_ref=r2.at[block_of(peer if incoming else me)],
            send_sem=s2_send.at[peer], recv_sem=s2_recv.at[peer if incoming else me],
            device_id=(peer, lat), device_id_type=MESH,
        )

    loop(1, blocks, lambda k: copy2(k, False).start())
    r2[block_of(me), :] = s2[block_of(me), :]
    loop(1, blocks, lambda k: copy2(k, True).wait_recv())

    def legendre(s):
        x = r2[pl.ds(s, blocks, stride=slots), :]
        turned = [x] + [pltpu.roll(x, shift=pad * k, axis=1) for k in range(1, 4)]
        high = [t.astype(BF16).astype(F32) for t in turned]
        low = [t - h for t, h in zip(turned, high)]
        lane = lax.broadcasted_iota(jnp.int32, x.shape, 1)
        operand = jnp.concatenate(
            [
                jnp.where(lane < pad, high[-q % 4], jnp.where(lane < 2 * pad, low[(1 - q) % 4], high[(2 - q) % 4]))
                for q in range(4)
            ],
            axis=0,
        ).astype(BF16)[:, : 3 * pad]
        pair = pair_ref[me * slots + s]
        step = 2 * cw
        for n in range(0, waves + cw, step):
            size = min(step, waves + cw - n)
            sums = jnp.dot(operand, cat[s, :, pl.ds(n, size)], preferred_element_type=F32)
            for k in range(size // cw):
                column = n + k * cw + lax.broadcasted_iota(jnp.int32, (levels, cw), 1)
                if n + k * cw == waves:
                    column = jnp.full((levels, cw), waves, jnp.int32)
                second = column >= waves - pair
                odd = (jnp.where(second, column + pair, column) & 1) == 1
                chosen = []
                for r in range(2):
                    pick = [
                        sums[(2 * w + r) * 2 * levels + p * levels :][:levels, k * cw : (k + 1) * cw]
                        for w in range(2)
                        for p in range(2)
                    ]
                    chosen.append(
                        jnp.where(second, jnp.where(odd, pick[3], pick[2]), jnp.where(odd, pick[1], pick[0]))
                    )
                if n + k * cw == waves:
                    side = lax.broadcasted_iota(jnp.int32, (levels, cw), 1) < cw // 2
                    part[s, pl.ds(main_rows, levels), :] = jnp.where(side, chosen[0], chosen[1])
                else:
                    for r in range(2):
                        row = (r * tiles + n // cw + k) * levels
                        part[s, pl.ds(row, levels), :] = chosen[r]

    def sib_copy(owner):
        return pltpu.make_async_remote_copy(
            src_ref=part.at[2 * owner + other], dst_ref=sib.at[owner], send_sem=sib_send.at[owner],
            recv_sem=sib_recv.at[owner], device_id=sibling, device_id_type=MESH,
        )

    def prepare(owner):
        legendre(2 * owner + other)
        sib_copy(owner).start()
        legendre(2 * owner + core)

    def ring_copy(way, t, p):
        low, rows, _ = pieces[p]
        slot = 2 * (at_z(hops - t) if way == 0 else at_z(t - hops)) + core
        return pltpu.make_async_remote_copy(
            src_ref=part.at[slot, pl.ds(low, rows)], dst_ref=ring.at[way, t, pl.ds(low, rows)],
            send_sem=rs_send.at[way, t, p], recv_sem=rs_recv.at[way, t, p],
            device_id=z_device(1 if way == 0 else -1), device_id_type=MESH,
        )

    def first_step(way, p):
        reach = pieces[p][2] if way == 0 else depth - 1 - pieces[p][2]
        return hops - reach

    def pass_on(way, t, p, received):
        low, rows, _ = pieces[p]
        owner = at_z(hops - t) if way == 0 else at_z(t - hops)
        value = part[2 * owner + core, pl.ds(low, rows), :] + sib[owner, pl.ds(low, rows), :]
        if received:
            ring_copy(way, t - 1, p).wait_recv()
            value = value + ring[way, t - 1, pl.ds(low, rows), :]
        part[2 * owner + core, pl.ds(low, rows), :] = value
        ring_copy(way, t, p).start()

    def prepare_step(t):
        for offset in sorted({hops - t, t - hops} if t else {hops}):
            prepare(at_z(offset))

    prepare_step(0)
    prepare_step(1)
    sib_copy_wait = lambda owner: sib_copy(owner).wait_recv()

    def reduce_step(t, begun):
        sib_copy_wait(at_z(hops - t))
        if begun > 0:
            sib_copy_wait(at_z(t - hops))
        for p in range(2):
            for way in range(2):
                first = first_step(way, p)
                if begun >= first:
                    pass_on(way, t, p, begun > first)

    reduce_step(0, 0)
    prepare_step(2)
    reduce_step(1, 1)

    def middle(t):
        prepare(at_z(hops - 1 - t))
        prepare(at_z(t + 1 - hops))
        reduce_step(t, 2)

    if hops > 2:
        loop(2, hops - 1, middle)
        prepare_step(hops)
        reduce_step(hops - 1, 2)

    mine = 2 * z + core
    sib_copy_wait(z)
    pair = pair_ref[me * slots + mine]
    level_of = lax.broadcasted_iota(jnp.int32, (levels, cw), 0)
    strength = jnp.zeros((levels, cw), F32)
    for level in range(levels):
        strength = jnp.where(level_of == level, diff_ref[level], strength)

    def damping(column):
        degree = jnp.where(column >= waves - pair, column - 1, pair + column).astype(F32)
        ratio = degree * (degree + 1.0) / float((waves - 1) * waves)
        return 1.0 / (1.0 + strength * (ratio * ratio))

    def ag_copy(way, u, p):
        low, rows, _ = pieces[p]
        slot = 2 * at_z(-u if way == 0 else u) + core
        return pltpu.make_async_remote_copy(
            src_ref=final.at[slot, pl.ds(low, rows)], dst_ref=final.at[slot, pl.ds(low, rows)],
            send_sem=ag_send.at[way, u, p], recv_sem=ag_recv.at[way, u, p],
            device_id=z_device(1 if way == 0 else -1), device_id_type=MESH,
        )

    def as_copy(owner, p, side):
        low, rows, _ = pieces[p]
        slot = 2 * owner + side
        return pltpu.make_async_remote_copy(
            src_ref=final.at[slot, pl.ds(low, rows)], dst_ref=final.at[slot, pl.ds(low, rows)],
            send_sem=as_send.at[owner, p], recv_sem=as_recv.at[owner, p],
            device_id=sibling, device_id_type=MESH,
        )

    def reach(way, p):
        return pieces[p][2] if way == 0 else depth - 1 - pieces[p][2]

    for p in range(2):
        low, rows, _ = pieces[p]
        for way in range(2):
            ring_copy(way, hops - 1, p).wait_recv()
        for row in range(low, low + rows, levels):
            piece = pl.ds(row, levels)
            value = part[mine, piece, :] + sib[z, piece, :]
            value = value + ring[0, hops - 1, piece, :] + ring[1, hops - 1, piece, :]
            if row >= main_rows:
                column = jnp.full((levels, cw), waves, jnp.int32)
            else:
                first = (row // levels) % tiles * cw
                column = first + lax.broadcasted_iota(jnp.int32, (levels, cw), 1)
            final[mine, piece, :] = value * damping(column)
        for way in range(2):
            ag_copy(way, 0, p).start()
        as_copy(z, p, core).start()

    def spread(u, last):
        for p in range(2):
            for way in range(2):
                if last and reach(way, p) < hops:
                    continue
                ag_copy(way, u, p).wait_recv()
                if not last:
                    if reach(way, p) == hops:
                        ag_copy(way, u + 1, p).start()
                    else:

                        @pl.when(u + 1 < hops - 1)
                        def _():
                            ag_copy(way, u + 1, p).start()

                as_copy(at_z(-u - 1 if way == 0 else u + 1), p, core).start()

    loop(0, hops - 1, lambda u: spread(u, False))
    spread(hops - 1, True)

    def settle_owner(owner):
        sib_copy(owner).wait_send()
        for p in range(2):
            as_copy(owner, p, core).wait_send()
            as_copy(owner, p, other).wait_recv()

    loop(0, depth, settle_owner)
    whole = pltpu.make_async_copy(final, out_hbm, out_sem)
    whole.start()

    def settle_peer(k):
        send1(k).wait_send()
        copy2(k, False).wait_send()

    loop(1, blocks, settle_peer)
    for way in range(2):
        for p in range(2):
            count = reach(way, p)
            loop(hops - count, hops, lambda t: ring_copy(way, t, p).wait_send())
            loop(0, count, lambda u: ag_copy(way, u, p).wait_send())
    whole.wait()


def per_device(depth, vorticity, legendre_table, pair_slots, diffusion):
    levels, _, band, width = vorticity.shape
    slots, columns = legendre_table.shape[1:]
    blocks = lax.axis_size("lon")
    waves = columns - 1
    cw = min(128, waves)
    half, hops, tiles, pad = blocks // 2, depth // 2, waves // cw, 32
    rows = 2 * tiles * levels + levels
    dims = (blocks, depth, levels, band, width, slots, waves, cw)
    twid = jnp.asarray(twiddles(blocks, width, waves))
    dma = pltpu.SemaphoreType.DMA
    any_spec, smem = pl.BlockSpec(memory_space=pltpu.HBM), pl.BlockSpec(memory_space=pltpu.SMEM)
    raw = pl.pallas_call(
        functools.partial(kernel, dims),
        out_shape=jax.ShapeDtypeStruct((slots, rows, cw), F32),
        in_specs=[smem, smem, any_spec, any_spec, any_spec],
        out_specs=any_spec,
        scratch_shapes=[
            pltpu.VMEM((2 * levels * band, width), F32),
            pltpu.VMEM((tiles + 1, (band + 1) * slots, cw), F32),
            pltpu.VMEM((band * slots, 1), F32),
            pltpu.VMEM(twid.shape, F32),
            pltpu.VMEM((2, *twid.shape), BF16),
            pltpu.VMEM((slots, 3 * pad, waves + cw), BF16),
            pltpu.VMEM((blocks, band, width), F32),
            pltpu.VMEM((blocks, band, width), F32),
            pltpu.VMEM((waves // 2, 4 * pad), F32),
            pltpu.VMEM((waves // 2, 4 * pad), F32),
            pltpu.VMEM((waves // 2 + slots, 4 * pad), F32),
            pltpu.VMEM((slots, rows, cw), F32),
            pltpu.VMEM((depth, rows, cw), F32),
            pltpu.VMEM((2, hops, rows, cw), F32),
            pltpu.VMEM((slots, rows, cw), F32),
            dma((2,)),
            dma((tiles + 1,)),
            dma,
            dma((blocks,)),
            dma((blocks,)),
            dma((blocks,)),
            dma((blocks,)),
            dma((depth,)),
            dma((depth,)),
            dma((2, hops, 2)),
            dma((2, hops, 2)),
            dma((2, hops, 2)),
            dma((2, hops, 2)),
            dma((depth, 2)),
            dma((depth, 2)),
        ],
        compiler_params=pltpu.CompilerParams(
            collective_id=0, has_side_effects=True, vmem_limit_bytes=61 * 1024 * 1024
        ),
    )(
        pair_slots,
        diffusion,
        vorticity.reshape(2 * levels * band, width),
        legendre_table.reshape(band * slots, columns),
        twid,
    )
    main = raw[:, : 2 * tiles * levels].reshape(slots, 2, tiles, levels, cw)
    main = main.transpose(0, 3, 1, 2, 4).reshape(slots, levels, 2, waves)
    tail = raw[:, 2 * tiles * levels :]
    tail = jnp.stack([tail[:, :, 0:1], tail[:, :, cw // 2 : cw // 2 + 1]], axis=2)
    return jnp.concatenate([main, tail], axis=3)


def solution(mesh):
    placed = (P(None, None, "lat", "lon"), P("lat", "lon", None), P(), P())
    return jax.shard_map(
        functools.partial(per_device, mesh.shape["lat"] // 2),
        mesh=mesh,
        in_specs=placed,
        out_specs=P("lon", None, None, None),
        check_vma=False,
    )
```

time: 368 us -> 99.8 us (0.27)
  waiting for transfers between devices: 308 us -> 0 us
  Pallas kernels: 0 us -> 90.8 us
  matrix products: 15.7 us -> 0 us
  between operations: 13.5 us -> 0.04 us
  other arithmetic: 13.9 us -> 2.49 us
  local copies, waits for them, and re-layouts: 17 us -> 6.23 us
    psum x1 -> x0, waiting for transfers between devices: 214 us -> none  [per_device(): summed = lax.psum(band_partial, 'lat')]
    reduce_scatter x1 -> x0, waiting for transfers between devices: 93.1 us -> none  [per_device(): lax.psum_scatter(product * norm_scale, 'lon', scatter_dimension=0, tiled=...]
    pallas_call x0 -> x1, Pallas kernels: none -> 90.8 us  [per_device(): pl.pallas_call(functools.partial(kernel, dims), out_shape=jax.ShapeDtypeS...]
    dot_general x2 -> x0, matrix products: 15.7 us -> none  [the longest x1 8.98 us: legendre(): jnp.einsum('spwrlj,jsc->spwlrc', stacked, wave_table, precision=lax.Preci...]
    reshape x2 -> x1, local copies, waits for them, and re-layouts: 7.25 us -> 2.29 us  [per_device(): main = main.transpose(0, 3, 1, 2, 4).reshape(slots, levels, 2, waves)]
    another operation x1, local copies, waits for them, and re-layouts: 4.01 us -> 0.29 us  [per_device(): tail = jnp.stack([tail[:, :, 0:1], tail[:, :, cw // 2:cw // 2 + 1]], axis=2)]
  transfers between devices with their start and end apart: 2 -> 0, of which waited for: 2 -> 0; matrix products, arithmetic and copies ran while one was open for 1% -> 0% of each run, Pallas kernels for 0% -> 0%
where the time goes in v1:
time: 99.8 us; the launch traced here: 99.6 us
  Pallas kernels  90.8 us (91%)
  local copies, waits for them, and re-layouts  6.23 us (6%)
  other arithmetic  2.49 us (2%)
    pallas_call x1, Pallas kernels, per_device(): pl.pallas_call(functools.partial(kernel, dims), out_shape=jax.ShapeDtypeS...  90.8 us
    concatenate x1, other arithmetic, per_device(): return jnp.concatenate([main, tail], axis=3)  2.48 us
    reshape x1, local copies, waits for them, and re-layouts, per_device(): main = main.transpose(0, 3, 1, 2, 4).reshape(slots, levels, 2, waves)  2.29 us

profile of v1, /device:TPU:1, one launch (start us, length us, event | category | flops | bytes accessed | tf_op | source)
XLA Modules:
  0.0 99.6 jit_solution(10779497453929107973)
XLA Ops:
  0.0 90.8 %shard_map.55 = f32[32,136,128]{2,1,0:T(8,128)} custom-call(s32[512]{0:T(512)} %pair_ref.1, f32[8]{0:T(128)} %diff_ref.1, f32[384,192]{1,0:T(8,128)} %bitcast.11, f32[768,1025]{1,0:T(8,128)} %bitcast.10, f32[16,256,192]{2,1,0:T(8,128)} %constant.2.clone.twid_hbm), custom_call_target="tpu_custom_call" | custom-call | tf_op jit(solution)/shard_map/pallas_call | solution.py:451
  90.9 0.0 slice-start
  90.9 1.2 %fusion = (f32[32,8,1]{2,1,0:T(8,128)S(1)}, f32[32,8,1]{2,1,0:T(8,128)S(1)}) fusion(f32[32,136,128]{2,1,0:T(8,128)} %shard_map.55), kind=kLoop, calls=%fused_computation.2 | loop fusion | bytes 4096 | tf_op jit(solution)/shard_map/slice | solution.py:501
  92.1 0.5 slice-done
  92.6 1.7 %copy.13 = f32[32,8,2,8,128]{4,3,2,1,0:T(8,128)} copy(f32[32,8,2,8,128]{4,1,3,2,0:T(8,128)S(1)} %bitcast.9) | data formatting | bytes 4194304 | tf_op jit(solution)/shard_map/transpose | solution.py:499
  94.3 2.3 %reshape.15 = f32[32,8,2,1024]{3,2,1,0:T(2,128)S(1)} reshape(f32[32,8,2,8,128]{4,3,2,1,0:T(8,128)} %copy.13) | data formatting | bytes 4194304 | tf_op jit(solution)/shard_map/reshape | solution.py:499
  96.6 0.1 copy.14
  96.7 0.1 copy.15
  96.8 0.3 copy.16
  97.1 2.5 %pad_maximum_fusion = f32[32,8,2,1025]{3,2,1,0:T(2,128)} fusion(f32[32,8,2,1]{3,2,1,0:T(2,128)S(1)} %copy.16, f32[32,8,2,1024]{3,2,1,0:T(2,128)S(1)} %reshape.15), kind=kLoop, calls=%fused_computation | loop fusion | flops 524800 | bytes 4198400 | tf_op jit(solution)/shard_map/concatenate | solution.py:502
  (1 shorter events, 0.0 us)
Async XLA Ops:
  90.9 1.7 %slice-start = ((f32[32,136,128]{2,1,0:T(8,128)}), f32[32,128,128]{2,1,0:T(8,128)S(1)}, s32[]{:S(2)}) async-start(f32[32,136,128]{2,1,0:T(8,128)} %shard_map.55), calls=%async_computation | async-start | bytes 4194304 | tf_op jit(solution)/shard_map/slice | solution.py:498

commit v2 on v1

--- a/solution.py
+++ b/solution.py
@@ -77,7 +77,7 @@
 
 def kernel(
     dims, pair_ref, diff_ref, vort_hbm, table_hbm, twid_hbm, out_hbm,
-    vort, table, tail, twid, twid_split, cat, s1, r1, g, s2, r2, part, sib, ring, final,
+    vort, table, tail, twid, twid_split, cat, s1, r1, g, s2, r2, part, sib, ring, final, spread,
     load_sem, tab_sem, out_sem, s1_send, s1_recv, s2_send, s2_recv, sib_send, sib_recv,
     rs_send, rs_recv, ag_send, ag_recv, as_send, as_recv,
 ):
@@ -89,6 +89,14 @@
     main_rows = 2 * tiles * levels
     pieces = ((0, main_rows // 2, hops), (main_rows // 2, main_rows // 2 + levels, hops - 1))
 
+    meet = [c for c in (0, 1, 2, 4, 6) if c < hops]
+
+    def parent(d):
+        return max(c for c in meet if c < d)
+
+    def children(c):
+        return sorted((d for d in range(1, hops + 1) if parent(d) == c), reverse=True)
+
     me = lax.axis_index("lon")
     lat = lax.axis_index("lat")
     z, core = lat // 2, lat % 2
@@ -125,7 +133,8 @@
         return carry
 
     lax.fori_loop(1, blocks, greet, 0)
-    for target in (z_device(1), z_device(-1), sibling):
+    near = sorted({sign * (d - parent(d)) for d in range(1, hops + 1) for sign in (1, -1)})
+    for target in [z_device(step) for step in near] + [sibling]:
         pl.semaphore_signal(barrier, inc=1, device_id=target, device_id_type=MESH)
 
     load.wait()
@@ -135,7 +144,7 @@
         s1[level] = north + south
         s1[levels + level] = north - south
 
-    pl.semaphore_wait(barrier, blocks + 2)
+    pl.semaphore_wait(barrier, blocks + len(near))
 
     def send1(k):
         peer = lax.rem(me + k, blocks)
@@ -281,68 +290,68 @@
             recv_sem=sib_recv.at[owner], device_id=sibling, device_id_type=MESH,
         )
 
-    def prepare(owner):
-        legendre(2 * owner + other)
-        sib_copy(owner).start()
-        legendre(2 * owner + core)
-
-    def ring_copy(way, t, p):
+    def owner_at(way, d):
+        return at_z(d if way == 0 else -d)
+
+    def reach(way, p):
+        return pieces[p][2] if way == 0 else depth - 1 - pieces[p][2]
+
+    def prepare(d):
+        count = 2 if 0 < d < hops else 1
+
+        def one(i):
+            sign = 1 - 2 * lax.rem(i, count)
+            owner = at_z(sign * d)
+            away = i < count
+            slot = 2 * owner + jnp.where(away, other, core)
+            legendre(slot)
+
+            @pl.when(away)
+            def _():
+                sib_copy(owner).start()
+
+        loop(0, 2 * count, one)
+
+    def ring_copy(way, d, p):
         low, rows, _ = pieces[p]
-        slot = 2 * (at_z(hops - t) if way == 0 else at_z(t - hops)) + core
-        return pltpu.make_async_remote_copy(
-            src_ref=part.at[slot, pl.ds(low, rows)], dst_ref=ring.at[way, t, pl.ds(low, rows)],
-            send_sem=rs_send.at[way, t, p], recv_sem=rs_recv.at[way, t, p],
-            device_id=z_device(1 if way == 0 else -1), device_id_type=MESH,
-        )
-
-    def first_step(way, p):
-        reach = pieces[p][2] if way == 0 else depth - 1 - pieces[p][2]
-        return hops - reach
-
-    def pass_on(way, t, p, received):
-        low, rows, _ = pieces[p]
-        owner = at_z(hops - t) if way == 0 else at_z(t - hops)
-        value = part[2 * owner + core, pl.ds(low, rows), :] + sib[owner, pl.ds(low, rows), :]
-        if received:
-            ring_copy(way, t - 1, p).wait_recv()
-            value = value + ring[way, t - 1, pl.ds(low, rows), :]
-        part[2 * owner + core, pl.ds(low, rows), :] = value
-        ring_copy(way, t, p).start()
-
-    def prepare_step(t):
-        for offset in sorted({hops - t, t - hops} if t else {hops}):
-            prepare(at_z(offset))
-
-    prepare_step(0)
-    prepare_step(1)
-    sib_copy_wait = lambda owner: sib_copy(owner).wait_recv()
-
-    def reduce_step(t, begun):
-        sib_copy_wait(at_z(hops - t))
-        if begun > 0:
-            sib_copy_wait(at_z(t - hops))
+        slot = 2 * owner_at(way, d) + core
+        hop = d - parent(d)
+        return pltpu.make_async_remote_copy(
+            src_ref=part.at[slot, pl.ds(low, rows)], dst_ref=ring.at[way, d - 1, pl.ds(low, rows)],
+            send_sem=rs_send.at[way, d - 1, p], recv_sem=rs_recv.at[way, d - 1, p],
+            device_id=z_device(hop if way == 0 else -hop), device_id_type=MESH,
+        )
+
+    def pass_on(d):
+        sib_copy(owner_at(0, d)).wait_recv()
+        if d < hops:
+            sib_copy(owner_at(1, d)).wait_recv()
         for p in range(2):
+            low, rows, _ = pieces[p]
             for way in range(2):
-                first = first_step(way, p)
-                if begun >= first:
-                    pass_on(way, t, p, begun > first)
-
-    reduce_step(0, 0)
-    prepare_step(2)
-    reduce_step(1, 1)
-
-    def middle(t):
-        prepare(at_z(hops - 1 - t))
-        prepare(at_z(t + 1 - hops))
-        reduce_step(t, 2)
-
-    if hops > 2:
-        loop(2, hops - 1, middle)
-        prepare_step(hops)
-        reduce_step(hops - 1, 2)
+                if d > reach(way, p):
+                    continue
+                owner = owner_at(way, d)
+                value = part[2 * owner + core, pl.ds(low, rows), :] + sib[owner, pl.ds(low, rows), :]
+                for child in children(d) if d in meet else ():
+                    if child <= reach(way, p):
+                        ring_copy(way, child, p).wait_recv()
+                        value = value + ring[way, child - 1, pl.ds(low, rows), :]
+                part[2 * owner + core, pl.ds(low, rows), :] = value
+                ring_copy(way, d, p).start()
+
+    waiting = []
+    for d in range(hops, -1, -1):
+        prepare(d)
+        for late in list(waiting):
+            if late not in meet or not children(late) or late - d >= 2 or d == 0:
+                pass_on(late)
+                waiting.remove(late)
+        if d:
+            waiting.append(d)
 
     mine = 2 * z + core
-    sib_copy_wait(z)
+    sib_copy(z).wait_recv()
     pair = pair_ref[me * slots + mine]
     level_of = lax.broadcasted_iota(jnp.int32, (levels, cw), 0)
     strength = jnp.zeros((levels, cw), F32)
@@ -354,13 +363,14 @@
         ratio = degree * (degree + 1.0) / float((waves - 1) * waves)
         return 1.0 / (1.0 + strength * (ratio * ratio))
 
-    def ag_copy(way, u, p):
+    def ag_copy(way, d, p):
         low, rows, _ = pieces[p]
-        slot = 2 * at_z(-u if way == 0 else u) + core
+        hop = d - parent(d)
+        slot = 2 * owner_at(1 - way, parent(d)) + core
         return pltpu.make_async_remote_copy(
             src_ref=final.at[slot, pl.ds(low, rows)], dst_ref=final.at[slot, pl.ds(low, rows)],
-            send_sem=ag_send.at[way, u, p], recv_sem=ag_recv.at[way, u, p],
-            device_id=z_device(1 if way == 0 else -1), device_id_type=MESH,
+            send_sem=ag_send.at[way, d - 1, p], recv_sem=ag_recv.at[way, d - 1, p],
+            device_id=z_device(hop if way == 0 else -hop), device_id_type=MESH,
         )
 
     def as_copy(owner, p, side):
@@ -372,17 +382,34 @@
             device_id=sibling, device_id_type=MESH,
         )
 
-    def reach(way, p):
-        return pieces[p][2] if way == 0 else depth - 1 - pieces[p][2]
+    def go_on(way, d, p):
+        for child in children(d) if d in meet else ():
+            if child <= reach(way, p):
+                ag_copy(way, child, p).start()
+
+    def lay_out(slot, p):
+        low, rows, _ = pieces[p]
+        for k in range(tiles):
+            spread[slot, :, p, pl.ds(k * cw, cw)] = final[slot, pl.ds(low + k * levels, levels), :]
+        if p:
+            last = final[slot, pl.ds(main_rows, levels), :]
+            spread[slot, :, 0, pl.ds(waves, 1)] = last[:, 0:1]
+            spread[slot, :, 1, pl.ds(waves, 1)] = last[:, cw // 2 : cw // 2 + 1]
+
+    def out_copy(slot):
+        return pltpu.make_async_copy(spread.at[slot], out_hbm.at[slot], out_sem.at[slot])
 
     for p in range(2):
         low, rows, _ = pieces[p]
         for way in range(2):
-            ring_copy(way, hops - 1, p).wait_recv()
+            for child in children(0):
+                ring_copy(way, child, p).wait_recv()
         for row in range(low, low + rows, levels):
             piece = pl.ds(row, levels)
             value = part[mine, piece, :] + sib[z, piece, :]
-            value = value + ring[0, hops - 1, piece, :] + ring[1, hops - 1, piece, :]
+            for way in range(2):
+                for child in children(0):
+                    value = value + ring[way, child - 1, piece, :]
             if row >= main_rows:
                 column = jnp.full((levels, cw), waves, jnp.int32)
             else:
@@ -390,38 +417,38 @@
                 column = first + lax.broadcasted_iota(jnp.int32, (levels, cw), 1)
             final[mine, piece, :] = value * damping(column)
         for way in range(2):
-            ag_copy(way, 0, p).start()
+            go_on(way, 0, p)
         as_copy(z, p, core).start()
 
-    def spread(u, last):
+    def finish(d):
+        for way in range(2 if 0 < d < hops else 1):
+            owner = owner_at(way, d)
+            for p in range(2):
+                as_copy(owner, p, other).wait_recv()
+                lay_out(2 * owner + core, p)
+                lay_out(2 * owner + other, p)
+            out_copy(2 * owner + core).start()
+            out_copy(2 * owner + other).start()
+
+    done = [0]
+    order = sorted(range(1, hops + 1), key=lambda d: d - 1.5 * (d in meet and bool(children(d)) or d == hops))
+    for d in order:
         for p in range(2):
             for way in range(2):
-                if last and reach(way, p) < hops:
-                    continue
-                ag_copy(way, u, p).wait_recv()
-                if not last:
-                    if reach(way, p) == hops:
-                        ag_copy(way, u + 1, p).start()
-                    else:
-
-                        @pl.when(u + 1 < hops - 1)
-                        def _():
-                            ag_copy(way, u + 1, p).start()
-
-                as_copy(at_z(-u - 1 if way == 0 else u + 1), p, core).start()
-
-    loop(0, hops - 1, lambda u: spread(u, False))
-    spread(hops - 1, True)
+                if d <= reach(way, p):
+                    ag_copy(way, d, p).wait_recv()
+                    go_on(way, d, p)
+                    as_copy(owner_at(1 - way, d), p, core).start()
+        finish(done[-1])
+        done.append(d)
+    finish(done[-1])
 
     def settle_owner(owner):
         sib_copy(owner).wait_send()
         for p in range(2):
             as_copy(owner, p, core).wait_send()
-            as_copy(owner, p, other).wait_recv()
 
     loop(0, depth, settle_owner)
-    whole = pltpu.make_async_copy(final, out_hbm, out_sem)
-    whole.start()
 
     def settle_peer(k):
         send1(k).wait_send()
@@ -430,10 +457,10 @@
     loop(1, blocks, settle_peer)
     for way in range(2):
         for p in range(2):
-            count = reach(way, p)
-            loop(hops - count, hops, lambda t: ring_copy(way, t, p).wait_send())
-            loop(0, count, lambda u: ag_copy(way, u, p).wait_send())
-    whole.wait()
+            for d in range(1, reach(way, p) + 1):
+                ring_copy(way, d, p).wait_send()
+                ag_copy(way, d, p).wait_send()
+    loop(0, slots, lambda slot: out_copy(slot).wait())
 
 
 def per_device(depth, vorticity, legendre_table, pair_slots, diffusion):
@@ -448,9 +475,9 @@
     twid = jnp.asarray(twiddles(blocks, width, waves))
     dma = pltpu.SemaphoreType.DMA
     any_spec, smem = pl.BlockSpec(memory_space=pltpu.HBM), pl.BlockSpec(memory_space=pltpu.SMEM)
-    raw = pl.pallas_call(
+    return pl.pallas_call(
         functools.partial(kernel, dims),
-        out_shape=jax.ShapeDtypeStruct((slots, rows, cw), F32),
+        out_shape=jax.ShapeDtypeStruct((slots, levels, 2, columns), F32),
         in_specs=[smem, smem, any_spec, any_spec, any_spec],
         out_specs=any_spec,
         scratch_shapes=[
@@ -469,9 +496,10 @@
             pltpu.VMEM((depth, rows, cw), F32),
             pltpu.VMEM((2, hops, rows, cw), F32),
             pltpu.VMEM((slots, rows, cw), F32),
+            pltpu.VMEM((slots, levels, 2, columns), F32),
             dma((2,)),
             dma((tiles + 1,)),
-            dma,
+            dma((slots,)),
             dma((blocks,)),
             dma((blocks,)),
             dma((blocks,)),
@@ -495,11 +523,6 @@
         legendre_table.reshape(band * slots, columns),
         twid,
     )
-    main = raw[:, : 2 * tiles * levels].reshape(slots, 2, tiles, levels, cw)
-    main = main.transpose(0, 3, 1, 2, 4).reshape(slots, levels, 2, waves)
-    tail = raw[:, 2 * tiles * levels :]
-    tail = jnp.stack([tail[:, :, 0:1], tail[:, :, cw // 2 : cw // 2 + 1]], axis=2)
-    return jnp.concatenate([main, tail], axis=3)
 
 
 def solution(mesh):

time: 99.8 us -> 85.9 us (0.86)
  Pallas kernels: 90.8 us -> 81.9 us
  other arithmetic: 2.49 us -> 0 us
  local copies, waits for them, and re-layouts: 6.23 us -> 3.88 us
    pallas_call x1, Pallas kernels: 90.8 us -> 81.9 us  [per_device(): pl.pallas_call(functools.partial(kernel, dims), out_shape=jax.ShapeDtypeS...]
    unnamed x0 -> x1, local copies, waits for them, and re-layouts: none -> 3.88 us
    concatenate x1 -> x0, other arithmetic: 2.48 us -> none  [per_device(): return jnp.concatenate([main, tail], axis=3)]
    reshape x1 -> x0, local copies, waits for them, and re-layouts: 2.29 us -> none  [per_device(): main = main.transpose(0, 3, 1, 2, 4).reshape(slots, levels, 2, waves)]
    slice x5 -> x0, local copies, waits for them, and re-layouts: 1.96 us -> none  [the longest x3 1.46 us: per_device(): tail = jnp.stack([tail[:, :, 0:1], tail[:, :, cw // 2:cw // 2 + 1]], axis=2)]
    transpose x1 -> x0, local copies, waits for them, and re-layouts: 1.69 us -> none  [per_device(): main = main.transpose(0, 3, 1, 2, 4).reshape(slots, levels, 2, waves)]
where the time goes in v2:
time: 85.9 us; the launch traced here: 85.8 us
  Pallas kernels  81.9 us (95%)
  local copies, waits for them, and re-layouts  3.88 us (5%)
    pallas_call x1, Pallas kernels, per_device(): pl.pallas_call(functools.partial(kernel, dims), out_shape=jax.ShapeDtypeS...  81.9 us
    unnamed x1, local copies, waits for them, and re-layouts  3.88 us

profile of v2, /device:TPU:1, one launch (start us, length us, event | category | flops | bytes accessed | tf_op | source)
XLA Modules:
  0.0 85.8 jit_solution(2719227453030903606)
XLA Ops:
  0.0 81.9 %shard_map.55 = f32[32,8,2,1025]{3,2,1,0:T(2,128)} custom-call(s32[512]{0:T(512)} %pair_ref.1, f32[8]{0:T(128)} %diff_ref.1, f32[384,192]{1,0:T(8,128)} %bitcast.3, f32[768,1025]{1,0:T(8,128)} %bitcast.2, f32[16,256,192]{2,1,0:T(8,128)} %constant.2.clone.twid_hbm), custom_call_target="tpu_custom_call" | custom-call | tf_op jit(solution)/shard_map/pallas_call | solution.py:478
  81.9 3.9 %copy.7 = f32[32,8,2,1025]{3,2,1,0:T(2,128)} copy(f32[32,8,2,1025]{3,2,1,0:T(2,128)} %shard_map.55) | data formatting | bytes 4198400

commit v3 on v2

--- a/solution.py
+++ b/solution.py
@@ -10,6 +10,8 @@
 from jax.sharding import PartitionSpec as P
 
 MESH = pl.DeviceIdType.MESH
+CUTS = 1
+MEET = (0, 1, 2, 4, 6)
 F32 = jnp.float32
 BF16 = jnp.bfloat16
 
@@ -87,9 +89,12 @@
     pad = 32
     per_class = waves // 2 // blocks
     main_rows = 2 * tiles * levels
-    pieces = ((0, main_rows // 2, hops), (main_rows // 2, main_rows // 2 + levels, hops - 1))
-
-    meet = [c for c in (0, 1, 2, 4, 6) if c < hops]
+    cut = min(CUTS, tiles)
+    size = main_rows // 2 // cut
+    pieces = [(k * size, size, hops - k // cut) for k in range(2 * cut)]
+    pieces[-1] = (pieces[-1][0], size + levels, hops - 1)
+
+    meet = [c for c in MEET if c < hops]
 
     def parent(d):
         return max(c for c in meet if c < d)
@@ -185,8 +190,6 @@
             cat[s, pl.ds(pad, pad), lanes] = high
             cat[s, pl.ds(2 * pad, pad), lanes] = low
 
-    loop(0, slots, stack_table)
-
     load_twid.wait()
 
     def split_twiddles(k):
@@ -195,6 +198,7 @@
         twid_split[1, k] = low
 
     loop(0, 2 * half, split_twiddles)
+    loop(0, slots * 3 // 8, stack_table)
     loop(1, blocks, lambda k: recv1(k).wait_recv())
 
     spectrum = real_dft([r1[a] for a in range(blocks)])
@@ -240,6 +244,7 @@
 
     loop(1, blocks, lambda k: copy2(k, False).start())
     r2[block_of(me), :] = s2[block_of(me), :]
+    loop(slots * 3 // 8, slots, stack_table)
     loop(1, blocks, lambda k: copy2(k, True).wait_recv())
 
     def legendre(s):
@@ -326,7 +331,7 @@
         sib_copy(owner_at(0, d)).wait_recv()
         if d < hops:
             sib_copy(owner_at(1, d)).wait_recv()
-        for p in range(2):
+        for p in range(len(pieces)):
             low, rows, _ = pieces[p]
             for way in range(2):
                 if d > reach(way, p):
@@ -389,9 +394,10 @@
 
     def lay_out(slot, p):
         low, rows, _ = pieces[p]
-        for k in range(tiles):
-            spread[slot, :, p, pl.ds(k * cw, cw)] = final[slot, pl.ds(low + k * levels, levels), :]
-        if p:
+        for row in range(low, min(low + rows, main_rows), levels):
+            k = (row // levels) % tiles
+            spread[slot, :, row // (tiles * levels), pl.ds(k * cw, cw)] = final[slot, pl.ds(row, levels), :]
+        if low + rows > main_rows:
             last = final[slot, pl.ds(main_rows, levels), :]
             spread[slot, :, 0, pl.ds(waves, 1)] = last[:, 0:1]
             spread[slot, :, 1, pl.ds(waves, 1)] = last[:, cw // 2 : cw // 2 + 1]
@@ -399,7 +405,7 @@
     def out_copy(slot):
         return pltpu.make_async_copy(spread.at[slot], out_hbm.at[slot], out_sem.at[slot])
 
-    for p in range(2):
+    for p in range(len(pieces)):
         low, rows, _ = pieces[p]
         for way in range(2):
             for child in children(0):
@@ -423,7 +429,7 @@
     def finish(d):
         for way in range(2 if 0 < d < hops else 1):
             owner = owner_at(way, d)
-            for p in range(2):
+            for p in range(len(pieces)):
                 as_copy(owner, p, other).wait_recv()
                 lay_out(2 * owner + core, p)
                 lay_out(2 * owner + other, p)
@@ -433,7 +439,7 @@
     done = [0]
     order = sorted(range(1, hops + 1), key=lambda d: d - 1.5 * (d in meet and bool(children(d)) or d == hops))
     for d in order:
-        for p in range(2):
+        for p in range(len(pieces)):
             for way in range(2):
                 if d <= reach(way, p):
                     ag_copy(way, d, p).wait_recv()
@@ -445,7 +451,7 @@
 
     def settle_owner(owner):
         sib_copy(owner).wait_send()
-        for p in range(2):
+        for p in range(len(pieces)):
             as_copy(owner, p, core).wait_send()
 
     loop(0, depth, settle_owner)
@@ -456,11 +462,25 @@
 
     loop(1, blocks, settle_peer)
     for way in range(2):
-        for p in range(2):
+        for p in range(len(pieces)):
             for d in range(1, reach(way, p) + 1):
                 ring_copy(way, d, p).wait_send()
                 ag_copy(way, d, p).wait_send()
     loop(0, slots, lambda slot: out_copy(slot).wait())
+
+
+def hand_over(groups, source, target, held, in_sem, out_sem):
+    size = source.shape[0] // groups
+    parts = [pl.ds(k * size, size) for k in range(groups)]
+    reads = [pltpu.make_async_copy(source.at[at], held.at[at], in_sem.at[k]) for k, at in enumerate(parts)]
+    writes = [pltpu.make_async_copy(held.at[at], target.at[at], out_sem.at[k]) for k, at in enumerate(parts)]
+    for read in reads:
+        read.start()
+    for read, write in zip(reads, writes):
+        read.wait()
+        write.start()
+    for write in writes:
+        write.wait()
 
 
 def per_device(depth, vorticity, legendre_table, pair_slots, diffusion):
@@ -471,11 +491,12 @@
     cw = min(128, waves)
     half, hops, tiles, pad = blocks // 2, depth // 2, waves // cw, 32
     rows = 2 * tiles * levels + levels
+    count = 2 * min(CUTS, tiles)
     dims = (blocks, depth, levels, band, width, slots, waves, cw)
     twid = jnp.asarray(twiddles(blocks, width, waves))
     dma = pltpu.SemaphoreType.DMA
     any_spec, smem = pl.BlockSpec(memory_space=pltpu.HBM), pl.BlockSpec(memory_space=pltpu.SMEM)
-    return pl.pallas_call(
+    result = pl.pallas_call(
         functools.partial(kernel, dims),
         out_shape=jax.ShapeDtypeStruct((slots, levels, 2, columns), F32),
         in_specs=[smem, smem, any_spec, any_spec, any_spec],
@@ -506,12 +527,12 @@
             dma((blocks,)),
             dma((depth,)),
             dma((depth,)),
-            dma((2, hops, 2)),
-            dma((2, hops, 2)),
-            dma((2, hops, 2)),
-            dma((2, hops, 2)),
-            dma((depth, 2)),
-            dma((depth, 2)),
+            dma((2, hops, count)),
+            dma((2, hops, count)),
+            dma((2, hops, count)),
+            dma((2, hops, count)),
+            dma((depth, count)),
+            dma((depth, count)),
         ],
         compiler_params=pltpu.CompilerParams(
             collective_id=0, has_side_effects=True, vmem_limit_bytes=61 * 1024 * 1024
@@ -523,6 +544,15 @@
         legendre_table.reshape(band * slots, columns),
         twid,
     )
+    groups = 8
+    return pl.pallas_call(
+        functools.partial(hand_over, groups),
+        out_shape=jax.ShapeDtypeStruct(result.shape, F32),
+        in_specs=[any_spec],
+        out_specs=any_spec,
+        scratch_shapes=[pltpu.VMEM(result.shape, F32), dma((groups,)), dma((groups,))],
+        compiler_params=pltpu.CompilerParams(vmem_limit_bytes=61 * 1024 * 1024),
+    )(result)
 
 
 def solution(mesh):

time: 85.9 us -> 84.5 us (0.984)
  local copies, waits for them, and re-layouts: 3.88 us -> 0 us
  Pallas kernels: 81.9 us -> 84.4 us
    unnamed x1 -> x0, local copies, waits for them, and re-layouts: 3.88 us -> none
    pallas_call x0 -> x1, Pallas kernels: none -> 2.49 us  [per_device(): pl.pallas_call(functools.partial(hand_over, groups), out_shape=jax.ShapeD...]
where the time goes in v3:
time: 84.5 us; the launch traced here: 84.4 us
  Pallas kernels  84.4 us (100%)
    pallas_call x1, Pallas kernels, per_device(): pl.pallas_call(functools.partial(kernel, dims), out_shape=jax.ShapeDtypeS...  81.9 us
    pallas_call x1, Pallas kernels, per_device(): pl.pallas_call(functools.partial(hand_over, groups), out_shape=jax.ShapeD...  2.49 us

profile of v3, /device:TPU:1, one launch (start us, length us, event | category | flops | bytes accessed | tf_op | source)
XLA Modules:
  0.0 84.4 jit_solution(10184595896399165426)
XLA Ops:
  0.0 81.9 %shard_map.55.source = f32[32,8,2,1025]{3,2,1,0:T(2,128)} custom-call(s32[512]{0:T(512)} %pair_ref.1, f32[8]{0:T(128)} %diff_ref.1, f32[384,192]{1,0:T(8,128)} %bitcast.3, f32[768,1025]{1,0:T(8,128)} %bitcast.2, f32[16,256,192]{2,1,0:T(8,128)} %constant.2.clone.twid_hbm), custom_call_target="tpu_custom_call" | custom-call | tf_op jit(solution)/shard_map/pallas_call | solution.py:499
  81.9 2.5 %shard_map.56 = f32[32,8,2,1025]{3,2,1,0:T(2,128)} custom-call(f32[32,8,2,1025]{3,2,1,0:T(2,128)} %shard_map.55.source), custom_call_target="tpu_custom_call" | custom-call | tf_op jit(solution)/shard_map/pallas_call | solution.py:548

commit v4 on v3

--- a/solution.py
+++ b/solution.py
@@ -11,7 +11,7 @@
 
 MESH = pl.DeviceIdType.MESH
 CUTS = 1
-MEET = (0, 1, 2, 4, 6)
+MEET = (0, 2, 4, 6)
 F32 = jnp.float32
 BF16 = jnp.bfloat16
 
@@ -348,10 +348,11 @@
     waiting = []
     for d in range(hops, -1, -1):
         prepare(d)
-        for late in list(waiting):
-            if late not in meet or not children(late) or late - d >= 2 or d == 0:
-                pass_on(late)
-                waiting.remove(late)
+        alone = [late for late in waiting if late not in meet or not children(late)]
+        joined = [late for late in waiting if late not in alone and (d == 0 or late == meet[-1] and late - d >= 3)]
+        for late in alone + joined:
+            pass_on(late)
+            waiting.remove(late)
         if d:
             waiting.append(d)
 
@@ -409,12 +410,13 @@
         low, rows, _ = pieces[p]
         for way in range(2):
             for child in children(0):
-                ring_copy(way, child, p).wait_recv()
+                if child <= reach(way, p):
+                    ring_copy(way, child, p).wait_recv()
         for row in range(low, low + rows, levels):
             piece = pl.ds(row, levels)
             value = part[mine, piece, :] + sib[z, piece, :]
             for way in range(2):
-                for child in children(0):
+                for child in (c for c in children(0) if c <= reach(way, p)):
                     value = value + ring[way, child - 1, piece, :]
             if row >= main_rows:
                 column = jnp.full((levels, cw), waves, jnp.int32)

time: 84.5 us -> 81.2 us (0.961)
  Pallas kernels: 84.4 us -> 81 us
    pallas_call x1, Pallas kernels: 81.9 us -> 78.5 us  [per_device(): pl.pallas_call(functools.partial(kernel, dims), out_shape=jax.ShapeDtypeS...]
where the time goes in v4:
time: 81.2 us; the launch traced here: 81 us
  Pallas kernels  81 us (100%)
    pallas_call x1, Pallas kernels, per_device(): pl.pallas_call(functools.partial(kernel, dims), out_shape=jax.ShapeDtypeS...  78.5 us
    pallas_call x1, Pallas kernels, per_device(): pl.pallas_call(functools.partial(hand_over, groups), out_shape=jax.ShapeD...  2.49 us

profile of v4, /device:TPU:1, one launch (start us, length us, event | category | flops | bytes accessed | tf_op | source)
XLA Modules:
  0.0 81.0 jit_solution(15938064456682243019)
XLA Ops:
  0.0 78.5 %shard_map.55.source = f32[32,8,2,1025]{3,2,1,0:T(2,128)} custom-call(s32[512]{0:T(512)} %pair_ref.1, f32[8]{0:T(128)} %diff_ref.1, f32[384,192]{1,0:T(8,128)} %bitcast.3, f32[768,1025]{1,0:T(8,128)} %bitcast.2, f32[16,256,192]{2,1,0:T(8,128)} %constant.2.clone.twid_hbm), custom_call_target="tpu_custom_call" | custom-call | tf_op jit(solution)/shard_map/pallas_call | solution.py:501
  78.5 2.5 %shard_map.56 = f32[32,8,2,1025]{3,2,1,0:T(2,128)} custom-call(f32[32,8,2,1025]{3,2,1,0:T(2,128)} %shard_map.55.source), custom_call_target="tpu_custom_call" | custom-call | tf_op jit(solution)/shard_map/pallas_call | solution.py:550

commit v5 on v4

--- a/solution.py
+++ b/solution.py
@@ -198,7 +198,12 @@
         twid_split[1, k] = low
 
     loop(0, 2 * half, split_twiddles)
-    loop(0, slots * 3 // 8, stack_table)
+    def stack_tables(i):
+        for k in range(4):
+            stack_table(4 * i + k)
+
+    early = slots * 3 // 32
+    loop(0, early, stack_tables)
     loop(1, blocks, lambda k: recv1(k).wait_recv())
 
     spectrum = real_dft([r1[a] for a in range(blocks)])
@@ -244,50 +249,60 @@
 
     loop(1, blocks, lambda k: copy2(k, False).start())
     r2[block_of(me), :] = s2[block_of(me), :]
-    loop(slots * 3 // 8, slots, stack_table)
+    loop(early, slots // 4, stack_tables)
     loop(1, blocks, lambda k: copy2(k, True).wait_recv())
 
-    def legendre(s):
+    def operand_of(s):
         x = r2[pl.ds(s, blocks, stride=slots), :]
         turned = [x] + [pltpu.roll(x, shift=pad * k, axis=1) for k in range(1, 4)]
         high = [t.astype(BF16).astype(F32) for t in turned]
         low = [t - h for t, h in zip(turned, high)]
         lane = lax.broadcasted_iota(jnp.int32, x.shape, 1)
-        operand = jnp.concatenate(
+        return jnp.concatenate(
             [
                 jnp.where(lane < pad, high[-q % 4], jnp.where(lane < 2 * pad, low[(1 - q) % 4], high[(2 - q) % 4]))
                 for q in range(4)
             ],
             axis=0,
         ).astype(BF16)[:, : 3 * pad]
-        pair = pair_ref[me * slots + s]
+
+    def choose(s, pair, n, size, sums):
+        for k in range(size // cw):
+            column = n + k * cw + lax.broadcasted_iota(jnp.int32, (levels, cw), 1)
+            if n + k * cw == waves:
+                column = jnp.full((levels, cw), waves, jnp.int32)
+            second = column >= waves - pair
+            odd = (jnp.where(second, column + pair, column) & 1) == 1
+            chosen = []
+            for r in range(2):
+                pick = [
+                    sums[(2 * w + r) * 2 * levels + p * levels :][:levels, k * cw : (k + 1) * cw]
+                    for w in range(2)
+                    for p in range(2)
+                ]
+                chosen.append(
+                    jnp.where(second, jnp.where(odd, pick[3], pick[2]), jnp.where(odd, pick[1], pick[0]))
+                )
+            if n + k * cw == waves:
+                side = lax.broadcasted_iota(jnp.int32, (levels, cw), 1) < cw // 2
+                part[s, pl.ds(main_rows, levels), :] = jnp.where(side, chosen[0], chosen[1])
+            else:
+                for r in range(2):
+                    row = (r * tiles + n // cw + k) * levels
+                    part[s, pl.ds(row, levels), :] = chosen[r]
+
+    def legendre(some):
+        operands = [operand_of(s) for s in some]
+        pairs = [pair_ref[me * slots + s] for s in some]
         step = 2 * cw
         for n in range(0, waves + cw, step):
             size = min(step, waves + cw - n)
-            sums = jnp.dot(operand, cat[s, :, pl.ds(n, size)], preferred_element_type=F32)
-            for k in range(size // cw):
-                column = n + k * cw + lax.broadcasted_iota(jnp.int32, (levels, cw), 1)
-                if n + k * cw == waves:
-                    column = jnp.full((levels, cw), waves, jnp.int32)
-                second = column >= waves - pair
-                odd = (jnp.where(second, column + pair, column) & 1) == 1
-                chosen = []
-                for r in range(2):
-                    pick = [
-                        sums[(2 * w + r) * 2 * levels + p * levels :][:levels, k * cw : (k + 1) * cw]
-                        for w in range(2)
-                        for p in range(2)
-                    ]
-                    chosen.append(
-                        jnp.where(second, jnp.where(odd, pick[3], pick[2]), jnp.where(odd, pick[1], pick[0]))
-                    )
-                if n + k * cw == waves:
-                    side = lax.broadcasted_iota(jnp.int32, (levels, cw), 1) < cw // 2
-                    part[s, pl.ds(main_rows, levels), :] = jnp.where(side, chosen[0], chosen[1])
-                else:
-                    for r in range(2):
-                        row = (r * tiles + n // cw + k) * levels
-                        part[s, pl.ds(row, levels), :] = chosen[r]
+            sums = [
+                jnp.dot(operand, cat[s, :, pl.ds(n, size)], preferred_element_type=F32)
+                for s, operand in zip(some, operands)
+            ]
+            for s, pair, value in zip(some, pairs, sums):
+                choose(s, pair, n, size, value)
 
     def sib_copy(owner):
         return pltpu.make_async_remote_copy(
@@ -302,20 +317,15 @@
         return pieces[p][2] if way == 0 else depth - 1 - pieces[p][2]
 
     def prepare(d):
-        count = 2 if 0 < d < hops else 1
-
         def one(i):
-            sign = 1 - 2 * lax.rem(i, count)
-            owner = at_z(sign * d)
-            away = i < count
-            slot = 2 * owner + jnp.where(away, other, core)
-            legendre(slot)
-
-            @pl.when(away)
-            def _():
-                sib_copy(owner).start()
-
-        loop(0, 2 * count, one)
+            owner = at_z(d - 2 * d * i)
+            legendre([2 * owner + other, 2 * owner + core])
+            sib_copy(owner).start()
+
+        if 0 < d < hops:
+            loop(0, 2, one)
+        else:
+            one(0)
 
     def ring_copy(way, d, p):
         low, rows, _ = pieces[p]

time: 81.2 us -> 81.4 us (level)
  no operation moved by 1% of the time
where the time goes in v5:
time: 81.4 us; the launch traced here: 81.3 us
  Pallas kernels  81.3 us (100%)
    pallas_call x1, Pallas kernels, per_device(): pl.pallas_call(functools.partial(kernel, dims), out_shape=jax.ShapeDtypeS...  78.8 us
    pallas_call x1, Pallas kernels, per_device(): pl.pallas_call(functools.partial(hand_over, groups), out_shape=jax.ShapeD...  2.49 us

profile of v5, /device:TPU:1, one launch (start us, length us, event | category | flops | bytes accessed | tf_op | source)
XLA Modules:
  0.0 81.3 jit_solution(14569419333739029650)
XLA Ops:
  0.0 78.8 %shard_map.55.source = f32[32,8,2,1025]{3,2,1,0:T(2,128)} custom-call(s32[512]{0:T(512)} %pair_ref.1, f32[8]{0:T(128)} %diff_ref.1, f32[384,192]{1,0:T(8,128)} %bitcast.3, f32[768,1025]{1,0:T(8,128)} %bitcast.2, f32[16,256,192]{2,1,0:T(8,128)} %constant.2.clone.twid_hbm), custom_call_target="tpu_custom_call" | custom-call | tf_op jit(solution)/shard_map/pallas_call | solution.py:511
  78.8 2.5 %shard_map.56 = f32[32,8,2,1025]{3,2,1,0:T(2,128)} custom-call(f32[32,8,2,1025]{3,2,1,0:T(2,128)} %shard_map.55.source), custom_call_target="tpu_custom_call" | custom-call | tf_op jit(solution)/shard_map/pallas_call | solution.py:560

commit v6 on v5

--- a/solution.py
+++ b/solution.py
@@ -219,8 +219,10 @@
             high, low = split(value)
             w_high = twid_split[0, number, pl.ds(0, count), :]
             w_low = twid_split[1, number, pl.ds(0, count), :]
-            term = dot_t(w_high, high) + (dot_t(w_high, low) + dot_t(w_low, high))
-            total = term if total is None else total + term
+            both = dot_t(w_high, jnp.concatenate([high, low], axis=0))
+            cross = dot_t(w_low, high)
+            total = (both, cross) if total is None else (total[0] + both, total[1] + cross)
+        total = total[0][:, :pad] + (total[0][:, pad:] + total[1])
         for at, (second, residue, which, _) in enumerate(rows):
             g[pl.ds(residue * per_class, per_class), pl.ds((2 * second + which) * pad, pad)] = total[
                 at * per_class : (at + 1) * per_class

time: 81.4 us -> 81 us (level)
  no operation moved by 1% of the time
where the time goes in v6:
time: 81 us; the launch traced here: 80.8 us
  Pallas kernels  80.8 us (100%)
    pallas_call x1, Pallas kernels, per_device(): pl.pallas_call(functools.partial(kernel, dims), out_shape=jax.ShapeDtypeS...  78.3 us
    pallas_call x1, Pallas kernels, per_device(): pl.pallas_call(functools.partial(hand_over, groups), out_shape=jax.ShapeD...  2.49 us

profile of v6, /device:TPU:1, one launch (start us, length us, event | category | flops | bytes accessed | tf_op | source)
XLA Modules:
  0.0 80.8 jit_solution(13011160016144172442)
XLA Ops:
  0.0 78.3 %shard_map.55.source = f32[32,8,2,1025]{3,2,1,0:T(2,128)} custom-call(s32[512]{0:T(512)} %pair_ref.1, f32[8]{0:T(128)} %diff_ref.1, f32[384,192]{1,0:T(8,128)} %bitcast.3, f32[768,1025]{1,0:T(8,128)} %bitcast.2, f32[16,256,192]{2,1,0:T(8,128)} %constant.2.clone.twid_hbm), custom_call_target="tpu_custom_call" | custom-call | tf_op jit(solution)/shard_map/pallas_call | solution.py:513
  78.3 2.5 %shard_map.56 = f32[32,8,2,1025]{3,2,1,0:T(2,128)} custom-call(f32[32,8,2,1025]{3,2,1,0:T(2,128)} %shard_map.55.source), custom_call_target="tpu_custom_call" | custom-call | tf_op jit(solution)/shard_map/pallas_call | solution.py:562
